TPU v7x, 512 devices: a whole 4x8x8 slice. The times are simulated.
512 devices in a mesh: batch: 32 (over z, x), blk: 16 (over y, core).
Axes of the slice: x: 4, y: 8, z: 8, core: 2. Of those that a mesh axis runs over, the one named last changes fastest.
Arguments:
- points: float32 [1024, 16, 3, 256], P('batch', 'blk'), may hold values from -6 to 6
- centers: float32 [1024, 16, 3, 384], P('batch', 'blk'), may hold values from -6 to 6
- exponents: float32 [1024, 16, 384], P('batch', 'blk'), may hold values from 0.1 to 1
- angular: float32 [1024, 16, 3, 384], P('batch', 'blk'), may hold values from -3 to 3
- grid_weights: float32 [1024, 16, 256], P('batch', 'blk'), may hold values from 0.001 to 0.01
- hartree: float32 [1024, 16, 256], P('batch', 'blk'), may hold values from 0 to 1.7
- load_plan: int32 [16, 1024], P('blk'), may hold values from 0 to 1023, each once within a row
- density_blocks: bfloat16 [256, 128, 128], P('blk'), may hold values from -0.046875 to 0.046875
- pair_lists: int32 [32, 16, 16, 2], P('batch', 'blk'), may hold values from 0 to 15
- batch_pairs: int32 [1024, 16, 9], P('batch', 'blk'), may hold values from 0 to 31, as said below
Outputs:
- hamiltonian: float32 [256, 128, 128], P('blk')
- density: float32 [1024, 16, 256], P('batch', 'blk')
Inputs may be any that keep to these rules, and one draw needn't show every extreme that they name: Each row of load_plan names every storage row of its column once. `pair_lists`: local index of a block pair within the 16 pairs held by one index of blk. `batch_pairs`: entry e of a device's table is the (e % 2)-th block it reads from index e // 2 of blk; every entry of a device's table is named by some pair of its batches.
All inputs are finite; a program needn't handle non-finite values.
Results may differ from a plain program's by a relative error of at most 0.0065.
Values may be sent and summed in bfloat16 or wider, within the bound.
No kernel may reach another device: no remote copies, remote signals or barrier semaphores. Data moves between devices by JAX's collectives and lax.ppermute only.
A program may use at most 64 MiB of HBM per device.

v0:
```python
import jax
import jax.numpy as jnp
from jax import lax
from jax.sharding import PartitionSpec as P

LIST = 3
xc_scale = 0.98474502
soft_square = 0.01


def exchange_potential(grid_rho):
    return -xc_scale * jnp.power(grid_rho * grid_rho + soft_square, 1.0 / 6.0)


def evaluate(points, centers, exponents, angular):
    distance = jnp.zeros(points.shape[:-2] + (points.shape[-1], centers.shape[-1]), jnp.float32)
    angular_part = jnp.ones_like(distance)
    for component in range(3):
        delta = points[..., component, :, None] - centers[..., component, None, :]
        distance = distance + delta * delta
        angular_part = angular_part + angular[..., component, None, :] * delta
    return (jnp.exp(-exponents[..., None, :] * distance) * angular_part).astype(jnp.bfloat16)


def on_device(
    points,
    centers,
    exponents,
    angular,
    grid_weights,
    hartree,
    load_plan,
    density_blocks,
    pair_lists,
    batch_pairs,
):
    slot_count = points.shape[0]
    grid_size = points.shape[3]
    columns = lax.axis_size("blk")
    per_owner = pair_lists.shape[3]
    held_pairs = density_blocks.shape[0]
    block_size = density_blocks.shape[1]
    entries = columns * per_owner
    list_size = LIST
    basis_width = list_size * block_size
    batch_rank = lax.axis_index("batch")
    plan_rows = lax.dynamic_slice_in_dim(load_plan[0], batch_rank * slot_count, slot_count)
    stored = lax.all_gather(hartree[:, 0, :], "batch", axis=0, tiled=True)
    potential = stored[plan_rows]
    wanted = pair_lists[0, 0]
    asked_slots = lax.all_to_all(wanted, "blk", split_axis=0, concat_axis=0, tiled=True)
    owner_base = jnp.arange(entries, dtype=jnp.int32) // per_owner * held_pairs
    global_ids = owner_base + wanted.reshape(entries)
    blank_table = jnp.zeros((entries, block_size, block_size), jnp.bfloat16)
    piece = lax.all_gather(density_blocks, "blk", axis=0, tiled=True)
    inside = (global_ids >= 0) & (global_ids < piece.shape[0])
    chosen = piece[jnp.clip(global_ids, 0, piece.shape[0] - 1)]
    fetched = jnp.where(inside[:, None, None], chosen, blank_table)
    group_size = 4
    loop_turns = slot_count // group_size

    def take_rows(value, turn_index):
        return lax.dynamic_slice_in_dim(value, turn_index * group_size, group_size, 0)

    def integrate(partial_table, turn_index):
        basis = evaluate(
            take_rows(points, turn_index)[:, 0],
            take_rows(centers, turn_index)[:, 0],
            take_rows(exponents, turn_index)[:, 0],
            take_rows(angular, turn_index)[:, 0],
        )
        slot_refs = take_rows(batch_pairs, turn_index)[:, 0]
        blocks = fetched[slot_refs]
        sub_density = (
            blocks.reshape(group_size, list_size, list_size, block_size, block_size)
            .transpose(0, 1, 3, 2, 4)
            .reshape(group_size, basis_width, basis_width)
        )
        inner = jnp.einsum("gpm,gmn->gpn", basis, sub_density, preferred_element_type=jnp.float32)
        grid_rho = jnp.sum(inner * basis.astype(jnp.float32), axis=-1)
        effective = take_rows(potential, turn_index) + exchange_potential(grid_rho)
        weight_rows = take_rows(grid_weights, turn_index)[:, 0]
        scaled = ((weight_rows * effective)[..., None] * basis.astype(jnp.float32)).astype(
            jnp.bfloat16
        )
        full_blocks = jnp.einsum("gpm,gpn->gmn", basis, scaled, preferred_element_type=jnp.float32)
        contributions = (
            full_blocks.reshape(group_size, list_size, block_size, list_size, block_size)
            .transpose(0, 1, 3, 2, 4)
            .reshape(group_size * list_size * list_size, block_size, block_size)
        )
        partial_table = partial_table.at[slot_refs.reshape(-1)].add(contributions)
        return (partial_table, grid_rho)

    zero_table = jnp.zeros((entries, block_size, block_size), jnp.float32)
    partial_table, rho_groups = lax.scan(integrate, zero_table, jnp.arange(loop_turns))
    grid_rho = rho_groups.reshape(slot_count, grid_size)
    received = lax.all_to_all(
        partial_table.reshape(columns, per_owner, block_size, block_size),
        "blk",
        split_axis=0,
        concat_axis=0,
        tiled=True,
    )
    owned_sums = (
        jnp.zeros((held_pairs, block_size, block_size), jnp.float32)
        .at[asked_slots.reshape(entries)]
        .add(received.reshape(entries, block_size, block_size))
    )
    hamiltonian = lax.psum(owned_sums, "batch")
    batch_total = load_plan.shape[1]
    placement = (plan_rows[None, :] == jnp.arange(batch_total, dtype=jnp.int32)[:, None]).astype(
        jnp.float32
    )
    spread_rows = jnp.dot(
        placement, grid_rho, precision=lax.Precision.HIGHEST, preferred_element_type=jnp.float32
    )
    density = lax.psum_scatter(spread_rows, "batch", scatter_dimension=0, tiled=True)
    return (hamiltonian, density[:, None, :])


def solution(mesh):
    return jax.shard_map(
        on_device,
        mesh=mesh,
        in_specs=(
            P("batch", "blk", None, None),
            P("batch", "blk", None, None),
            P("batch", "blk", None),
            P("batch", "blk", None, None),
            P("batch", "blk", None),
            P("batch", "blk", None),
            P("blk", None),
            P("blk", None, None),
            P("batch", "blk", None, None),
            P("batch", "blk", None),
        ),
        out_specs=(P("blk", None, None), P("batch", "blk", None)),
        check_vma=False,
    )
```

profile of v0, /device:TPU:8, one launch (start us, length us, event | category | flops | bytes accessed | tf_op | source)
XLA Modules:
  0.0 800.7 jit_solution(2311108223574678586)
XLA Ops:
  7.2 1.4 copy.57
  9.4 1.3 copy.56
  10.7 9.1 %all-to-all-start = ((s32[16,1,2]{2,1,0:T(1,128)}), s32[16,1,2]{2,1,0:T(1,128)S(1)}, u32[]{:S(2)}, u32[]{:S(2)}) async-start(s32[16,1,2]{2,1,0:T(1,128)} %copy.56), calls=%async_computation | async-start | bytes 16384 | tf_op jit(solution)/shard_map/all_to_all | solution.py:51
  22.3 76.3 %all-gather.6.cloned.1.call-done = f32[1024,1,256]{2,0,1:T(8,128)} async-done(((f32[32,1,256]{2,0,1:T(8,128)}), f32[1024,1,256]{2,0,1:T(8,128)}) %all-gather.6.cloned.1.call-update) | async-done | bytes 1048592 | tf_op jit(solution)/shard_map/all_gather | solution.py:48
  98.6 1.8 gather_fusion.1
  100.4 54.4 %all-gather.4.cloned.1.call-done = bf16[256,128,128]{2,1,0:T(8,128)(2,1)} async-done(((bf16[16,128,128]{2,1,0:T(8,128)(2,1)}), bf16[256,128,128]{2,1,0:T(8,128)(2,1)}) %all-gather.4.cloned.1.call-update) | async-done | bytes 8388624 | tf_op jit(solution)/shard_map/all_gather | solution.py:55
  154.8 4.1 gather_fusion.2
  159.1 1.5 broadcast_in_dim.40
  160.6 234.9 %while.12 = (s32[]{:T(128)}, f32[32,128,128]{2,1,0:T(8,128)}, f32[8,4,256]{2,1,0:T(4,128)S(1)}, s32[8]{0:T(128)S(1)}, s32[32,1,9]{2,0,1:T(8,128)S(1)}, /*index=5...) while((s32[]{:T(128)}, f32[32,128,128]{2,1,0:T(8,128)}, ...), condition=%wide.region_3.4_spmd, body=%wide.region_0.3_spmd.sunk | while | flops 633674496 | bytes 35997664 | solution.py:96
  165.4 1.1 reshape.301
  167.2 2.9 fusion.49
  170.8 4.2 fusion.51
  175.1 3.5 reshape.302
  178.5 1.7 copy.100
  180.3 9.6 %scatter_fusion = f32[32,128,128]{2,1,0:T(8,128)} fusion(f32[32,128,128]{2,1,0:T(8,128)} %get-tuple-element.276, s32[36]{0:T(128)S(1)} %fusion.47, f32[36,128,128]{2,1,0:T(8,128)} %bitcast.106), kind=kCustom, calls=%fused_computation.3.clone.1 | custom fusion | flops 589824 | bytes 7078032 | tf_op jit(solution)/shard_map/while/body/eval_jaxpr/scatter-add | solution.py:92
  194.8 1.1 reshape.301
  196.6 2.9 fusion.49
  200.2 4.2 fusion.51
  204.4 3.5 reshape.302
  207.9 1.7 copy.100
  209.7 9.7 %scatter_fusion = f32[32,128,128]{2,1,0:T(8,128)} fusion(f32[32,128,128]{2,1,0:T(8,128)} %get-tuple-element.276, s32[36]{0:T(128)S(1)} %fusion.47, f32[36,128,128]{2,1,0:T(8,128)} %bitcast.106), kind=kCustom, calls=%fused_computation.3.clone.1 | custom fusion | flops 589824 | bytes 7078032 | tf_op jit(solution)/shard_map/while/body/eval_jaxpr/scatter-add | solution.py:92
  224.2 1.1 reshape.301
  226.0 2.9 fusion.49
  229.6 4.2 fusion.51
  233.8 3.5 reshape.302
  237.3 1.7 copy.100
  239.1 9.7 %scatter_fusion = f32[32,128,128]{2,1,0:T(8,128)} fusion(f32[32,128,128]{2,1,0:T(8,128)} %get-tuple-element.276, s32[36]{0:T(128)S(1)} %fusion.47, f32[36,128,128]{2,1,0:T(8,128)} %bitcast.106), kind=kCustom, calls=%fused_computation.3.clone.1 | custom fusion | flops 589824 | bytes 7078032 | tf_op jit(solution)/shard_map/while/body/eval_jaxpr/scatter-add | solution.py:92
  253.6 1.1 reshape.301
  255.4 2.9 fusion.49
  259.0 4.2 fusion.51
  263.2 3.5 reshape.302
  266.7 1.7 copy.100
  268.5 9.7 %scatter_fusion = f32[32,128,128]{2,1,0:T(8,128)} fusion(f32[32,128,128]{2,1,0:T(8,128)} %get-tuple-element.276, s32[36]{0:T(128)S(1)} %fusion.47, f32[36,128,128]{2,1,0:T(8,128)} %bitcast.106), kind=kCustom, calls=%fused_computation.3.clone.1 | custom fusion | flops 589824 | bytes 7078032 | tf_op jit(solution)/shard_map/while/body/eval_jaxpr/scatter-add | solution.py:92
  283.0 1.1 reshape.301
  284.8 2.9 fusion.49
  288.4 4.2 fusion.51
  292.6 3.5 reshape.302
  296.1 1.7 copy.100
  297.9 9.7 %scatter_fusion = f32[32,128,128]{2,1,0:T(8,128)} fusion(f32[32,128,128]{2,1,0:T(8,128)} %get-tuple-element.276, s32[36]{0:T(128)S(1)} %fusion.47, f32[36,128,128]{2,1,0:T(8,128)} %bitcast.106), kind=kCustom, calls=%fused_computation.3.clone.1 | custom fusion | flops 589824 | bytes 7078032 | tf_op jit(solution)/shard_map/while/body/eval_jaxpr/scatter-add | solution.py:92
  312.4 1.1 reshape.301
  314.2 2.9 fusion.49
  317.8 4.2 fusion.51
  322.0 3.5 reshape.302
  325.5 1.7 copy.100
  327.3 9.6 %scatter_fusion = f32[32,128,128]{2,1,0:T(8,128)} fusion(f32[32,128,128]{2,1,0:T(8,128)} %get-tuple-element.276, s32[36]{0:T(128)S(1)} %fusion.47, f32[36,128,128]{2,1,0:T(8,128)} %bitcast.106), kind=kCustom, calls=%fused_computation.3.clone.1 | custom fusion | flops 589824 | bytes 7078032 | tf_op jit(solution)/shard_map/while/body/eval_jaxpr/scatter-add | solution.py:92
  343.5 2.9 fusion.49
  347.1 4.2 fusion.51
  351.3 3.5 reshape.302
  354.8 1.7 copy.100
  356.6 9.6 %scatter_fusion = f32[32,128,128]{2,1,0:T(8,128)} fusion(f32[32,128,128]{2,1,0:T(8,128)} %get-tuple-element.276, s32[36]{0:T(128)S(1)} %fusion.47, f32[36,128,128]{2,1,0:T(8,128)} %bitcast.106), kind=kCustom, calls=%fused_computation.3.clone.1 | custom fusion | flops 589824 | bytes 7078032 | tf_op jit(solution)/shard_map/while/body/eval_jaxpr/scatter-add | solution.py:92
  371.1 1.1 reshape.301
  372.8 2.9 fusion.49
  376.5 4.2 fusion.51
  380.7 3.5 reshape.302
  384.2 1.7 copy.100
  386.0 9.6 %scatter_fusion = f32[32,128,128]{2,1,0:T(8,128)} fusion(f32[32,128,128]{2,1,0:T(8,128)} %get-tuple-element.276, s32[36]{0:T(128)S(1)} %fusion.47, f32[36,128,128]{2,1,0:T(8,128)} %bitcast.106), kind=kCustom, calls=%fused_computation.3.clone.1 | custom fusion | flops 589824 | bytes 7078032 | tf_op jit(solution)/shard_map/while/body/eval_jaxpr/scatter-add | solution.py:92
  395.5 6.8 all-to-all-start.1
  403.2 1.5 fusion.21
  406.1 43.7 %all-to-all-done.1 = f32[16,2,128,128]{3,2,1,0:T(8,128)S(1)} async-done(((f32[16,2,128,128]{3,2,1,0:T(8,128)}), f32[16,2,128,128]{3,2,1,0:T(8,128)S(1)}, u32[]{:S(2)}, u32[]{:S(2)}) %all-to-all-start.1) | async-done | bytes 2097184 | tf_op jit(solution)/shard_map/all_to_all | solution.py:98
  449.9 2.7 scatter_fusion.1
  453.5 175.6 %reduce-scatter.2.cloned.1.call-done = f32[32,256]{1,0:T(8,128)} async-done(((f32[1024,256]{1,0:T(8,128)}), f32[32,256]{1,0:T(8,128)}) %reduce-scatter.2.cloned.1.call-update) | async-done | bytes 32784 | tf_op jit(solution)/shard_map/reduce_scatter | solution.py:118
  629.1 1.4 copy.66
  630.5 161.3 %all-reduce.2.cloned.1.call-done = f32[16,128,128]{2,1,0:T(8,128)} async-done(((f32[16,128,128]{2,1,0:T(8,128)}), f32[16,128,128]{2,1,0:T(8,128)}) %all-reduce.2.cloned.1.call-update) | async-done | bytes 1048592 | tf_op jit(solution)/shard_map/psum | solution.py:110
  791.8 2.3 copy.114
  (231 shorter events, 52.5 us)
Async XLA Ops:
  7.2 91.4 %all-gather.6.cloned.1.call-start = ((), (), s32[]{:S(2)}) async-start(), calls=%async_computation.6 | async-start | bytes 1081344 | tf_op jit(solution)/shard_map/all_gather | solution.py:48
  8.6 146.2 %all-gather.4.cloned.1.call-start = ((), (), s32[]{:S(2)}) async-start(), calls=%async_computation.3 | async-start | bytes 8912896 | tf_op jit(solution)/shard_map/all_gather | solution.py:55
  10.7 384.8 %all-to-all-start = ((s32[16,1,2]{2,1,0:T(1,128)}), s32[16,1,2]{2,1,0:T(1,128)S(1)}, u32[]{:S(2)}, u32[]{:S(2)}) async-start(s32[16,1,2]{2,1,0:T(1,128)} %copy.56), calls=%async_computation | async-start | bytes 16384 | tf_op jit(solution)/shard_map/all_to_all | solution.py:51
  160.6 3.8 copy-start
  180.3 9.6 %copy-start.1 = (bf16[32,128,128]{2,1,0:T(8,128)(2,1)S(1)}, bf16[32,128,128]{2,1,0:T(8,128)(2,1)}, u32[]{:S(2)}) copy-start(bf16[32,128,128]{2,1,0:T(8,128)(2,1)} %copy-done) | copy-start | bytes 3145732 | tf_op jit(solution)/shard_map/while
  190.0 3.8 copy-start
  209.7 9.7 %copy-start.1 = (bf16[32,128,128]{2,1,0:T(8,128)(2,1)S(1)}, bf16[32,128,128]{2,1,0:T(8,128)(2,1)}, u32[]{:S(2)}) copy-start(bf16[32,128,128]{2,1,0:T(8,128)(2,1)} %copy-done) | copy-start | bytes 3145732 | tf_op jit(solution)/shard_map/while
  219.4 3.8 copy-start
  239.1 9.7 %copy-start.1 = (bf16[32,128,128]{2,1,0:T(8,128)(2,1)S(1)}, bf16[32,128,128]{2,1,0:T(8,128)(2,1)}, u32[]{:S(2)}) copy-start(bf16[32,128,128]{2,1,0:T(8,128)(2,1)} %copy-done) | copy-start | bytes 3145732 | tf_op jit(solution)/shard_map/while
  248.8 3.8 copy-start
  268.5 9.8 %copy-start.1 = (bf16[32,128,128]{2,1,0:T(8,128)(2,1)S(1)}, bf16[32,128,128]{2,1,0:T(8,128)(2,1)}, u32[]{:S(2)}) copy-start(bf16[32,128,128]{2,1,0:T(8,128)(2,1)} %copy-done) | copy-start | bytes 3145732 | tf_op jit(solution)/shard_map/while
  278.2 3.8 copy-start
  297.9 9.7 %copy-start.1 = (bf16[32,128,128]{2,1,0:T(8,128)(2,1)S(1)}, bf16[32,128,128]{2,1,0:T(8,128)(2,1)}, u32[]{:S(2)}) copy-start(bf16[32,128,128]{2,1,0:T(8,128)(2,1)} %copy-done) | copy-start | bytes 3145732 | tf_op jit(solution)/shard_map/while
  307.6 3.8 copy-start
  327.3 9.6 %copy-start.1 = (bf16[32,128,128]{2,1,0:T(8,128)(2,1)S(1)}, bf16[32,128,128]{2,1,0:T(8,128)(2,1)}, u32[]{:S(2)}) copy-start(bf16[32,128,128]{2,1,0:T(8,128)(2,1)} %copy-done) | copy-start | bytes 3145732 | tf_op jit(solution)/shard_map/while
  336.9 3.8 copy-start
  356.6 9.6 %copy-start.1 = (bf16[32,128,128]{2,1,0:T(8,128)(2,1)S(1)}, bf16[32,128,128]{2,1,0:T(8,128)(2,1)}, u32[]{:S(2)}) copy-start(bf16[32,128,128]{2,1,0:T(8,128)(2,1)} %copy-done) | copy-start | bytes 3145732 | tf_op jit(solution)/shard_map/while
  366.3 3.8 copy-start
  386.0 9.6 %copy-start.1 = (bf16[32,128,128]{2,1,0:T(8,128)(2,1)S(1)}, bf16[32,128,128]{2,1,0:T(8,128)(2,1)}, u32[]{:S(2)}) copy-start(bf16[32,128,128]{2,1,0:T(8,128)(2,1)} %copy-done) | copy-start | bytes 3145732 | tf_op jit(solution)/shard_map/while
  395.5 54.2 %all-to-all-start.1 = ((f32[16,2,128,128]{3,2,1,0:T(8,128)}), f32[16,2,128,128]{3,2,1,0:T(8,128)S(1)}, u32[]{:S(2)}, u32[]{:S(2)}) async-start(f32[16,2,128,128]{3,2,1,0:T(8,128)} %bitcast.108), calls=%async_computation.1 | async-start | bytes 4194304 | tf_op jit(solution)/shard_map/all_to_all | solution.py:98
  402.4 226.8 %reduce-scatter.2.cloned.1.call-start = ((), (), s32[]{:S(2)}) async-start(), calls=%async_computation.5 | async-start | bytes 1081344 | tf_op jit(solution)/shard_map/reduce_scatter | solution.py:118
  404.7 387.1 %all-reduce.2.cloned.1.call-start = ((), (), s32[]{:S(2)}) async-start(), calls=%async_computation.4 | async-start | bytes 2097152 | tf_op jit(solution)/shard_map/psum | solution.py:110
  452.5 1.0 copy-start.2
Sparse Core Ops, SparseCore 0:
  11.7 86.7 all-gather.5
  100.7 54.0 all-gather.3
  407.6 221.4 reduce-scatter.1
  633.0 158.7 all-reduce.1
where the time goes:
time: 804 us; the launch traced here: 801 us
  waiting for transfers between devices  512 us (64%)
  local copies, waits for them, and re-layouts  112 us (14%)
  other arithmetic  81.9 us (10%)
  matrix products  58.4 us (7%)
  starting transfers between devices  16.1 us (2%)
  between operations  13.9 us (2%)
    reduce_scatter x1, waiting for transfers between devices, on_device(): lax.psum_scatter(spread_rows, 'batch', scatter_dimension=0, tiled=True)  176 us
    psum x1, waiting for transfers between devices, on_device(): hamiltonian = lax.psum(owned_sums, 'batch')  161 us
    scatter-add x8, other arithmetic, integrate(): partial_table = partial_table.at[slot_refs.reshape(-1)].add(contributions)  77.2 us
    all_gather x1, waiting for transfers between devices, on_device(): stored = lax.all_gather(hartree[:, 0, :], 'batch', axis=0, tiled=True)  76.3 us
    all_gather x1, waiting for transfers between devices, on_device(): piece = lax.all_gather(density_blocks, 'blk', axis=0, tiled=True)  54.4 us
    all_to_all x1, waiting for transfers between devices, on_device(): lax.all_to_all(partial_table.reshape(columns, per_owner, block_size, bloc...  43.7 us
    dot_general x8, matrix products, integrate(): jnp.einsum('gpm,gpn->gmn', basis, scaled, preferred_element_type=jnp.floa...  33.7 us
    reshape x8, local copies, waits for them, and re-layouts, integrate(): full_blocks.reshape(group_size, list_size, block_size, list_size, block_s...  27.7 us
  transfers between devices with their start and end apart: 6, of which 5 were waited for; matrix products, arithmetic and copies ran while one was open for 31% of the time, Pallas kernels for 0%

commit v1 on v0

--- a/solution.py
+++ b/solution.py
@@ -1,3 +1,4 @@
+import functools
 import jax
 import jax.numpy as jnp
 from jax import lax
@@ -6,6 +7,19 @@
 LIST = 3
 xc_scale = 0.98474502
 soft_square = 0.01
+
+
+def do_edge_in(incoming_x, lane_axis):
+    current_value = lax.all_to_all(
+        jnp.stack([incoming_x for _ in range(lax.axis_size(lane_axis))], axis=0),
+        concat_axis=0,
+        axis_name=lane_axis,
+        split_axis=0,
+    )
+    return jnp.concatenate(current_value, axis=0)
+
+
+supply_all_pairs_all = functools.partial(do_edge_in, lane_axis="blk")
 
 
 def exchange_potential(grid_rho):
@@ -52,7 +66,7 @@
     owner_base = jnp.arange(entries, dtype=jnp.int32) // per_owner * held_pairs
     global_ids = owner_base + wanted.reshape(entries)
     blank_table = jnp.zeros((entries, block_size, block_size), jnp.bfloat16)
-    piece = lax.all_gather(density_blocks, "blk", axis=0, tiled=True)
+    piece = supply_all_pairs_all(density_blocks)
     inside = (global_ids >= 0) & (global_ids < piece.shape[0])
     chosen = piece[jnp.clip(global_ids, 0, piece.shape[0] - 1)]
     fetched = jnp.where(inside[:, None, None], chosen, blank_table)

time: 804 us -> 864 us (1.075)
  waiting for transfers between devices: 512 us -> 560 us
    all_to_all x0 -> x1, waiting for transfers between devices: none -> 92.4 us  [do_edge_in(): lax.all_to_all(jnp.stack([incoming_x for _ in range(lax.axis_size(lane_ax...]
    all_gather x1 -> x0, waiting for transfers between devices: 54.4 us -> none  [on_device(): piece = lax.all_gather(density_blocks, 'blk', axis=0, tiled=True)]
    all_to_all x0 -> x1, starting transfers between devices: none -> 10.4 us  [do_edge_in(): lax.all_to_all(jnp.stack([incoming_x for _ in range(lax.axis_size(lane_ax...]
    all_gather x1, waiting for transfers between devices: 76.3 us -> 85.8 us  [on_device(): stored = lax.all_gather(hartree[:, 0, :], 'batch', axis=0, tiled=True)]
  transfers between devices with their start and end apart: 6 -> 6, of which waited for: 5 -> 5; matrix products, arithmetic and copies ran while one was open for 31% -> 29% of each run, Pallas kernels for 0% -> 0%
where the time goes in v1:
time: 864 us; the launch traced here: 860 us
  waiting for transfers between devices  560 us (65%)
  local copies, waits for them, and re-layouts  116 us (13%)
  other arithmetic  81.9 us (9%)
  matrix products  58.3 us (7%)
  starting transfers between devices  24.3 us (3%)
  between operations  13.9 us (2%)
    reduce_scatter x1, waiting for transfers between devices, on_device(): lax.psum_scatter(spread_rows, 'batch', scatter_dimension=0, tiled=True)  176 us
    psum x1, waiting for transfers between devices, on_device(): hamiltonian = lax.psum(owned_sums, 'batch')  161 us
    all_to_all x1, waiting for transfers between devices, do_edge_in(): lax.all_to_all(jnp.stack([incoming_x for _ in range(lax.axis_size(lane_ax...  92.4 us
    all_gather x1, waiting for transfers between devices, on_device(): stored = lax.all_gather(hartree[:, 0, :], 'batch', axis=0, tiled=True)  85.8 us
    scatter-add x8, other arithmetic, integrate(): partial_table = partial_table.at[slot_refs.reshape(-1)].add(contributions)  77.3 us
    all_to_all x1, waiting for transfers between devices, on_device(): lax.all_to_all(partial_table.reshape(columns, per_owner, block_size, bloc...  43.7 us
    dot_general x8, matrix products, integrate(): jnp.einsum('gpm,gpn->gmn', basis, scaled, preferred_element_type=jnp.floa...  33.6 us
    reshape x8, local copies, waits for them, and re-layouts, integrate(): full_blocks.reshape(group_size, list_size, block_size, list_size, block_s...  27.7 us
  transfers between devices with their start and end apart: 6, of which 5 were waited for; matrix products, arithmetic and copies ran while one was open for 29% of the time, Pallas kernels for 0%

profile of v1, /device:TPU:8, one launch (start us, length us, event | category | flops | bytes accessed | tf_op | source)
XLA Modules:
  0.0 860.0 jit_solution(5259896202348821484)
XLA Ops:
  7.2 6.4 stack.2
  13.6 10.4 %all-to-all-start.1 = ((bf16[16,16,128,128]{3,2,1,0:T(8,128)(2,1)}), bf16[16,16,128,128]{3,2,1,0:T(8,128)(2,1)}, u32[]{:S(2)}, u32[]{:S(2)}) async-start(bf16[16,16,128,128]{3,2,1,0:T(8,128)(2,1)} %stack.2), calls=%async_computation.1 | async-start | bytes 16777216 | tf_op jit(solution)/shard_map/all_to_all | solution.py:13
  26.6 85.8 %all-gather.3.cloned.1.call-done = f32[1024,1,256]{2,0,1:T(8,128)} async-done(((f32[32,1,256]{2,0,1:T(8,128)}), f32[1024,1,256]{2,0,1:T(8,128)}) %all-gather.3.cloned.1.call-update) | async-done | bytes 1048592 | tf_op jit(solution)/shard_map/all_gather | solution.py:62
  112.4 1.8 gather_fusion.1
  114.2 92.4 %all-to-all-done.1 = bf16[16,16,128,128]{3,2,1,0:T(8,128)(2,1)} async-done(((bf16[16,16,128,128]{3,2,1,0:T(8,128)(2,1)}), bf16[16,16,128,128]{3,2,1,0:T(8,128)(2,1)}, u32[]{:S(2)}, u32[]{:S(2)}) %all-to-all-start.1) | async-done | bytes 8388640 | tf_op jit(solution)/shard_map/all_to_all | solution.py:13
  206.7 6.4 all-to-all-start
  213.1 4.1 gather_fusion.2
  217.4 1.6 broadcast_in_dim.40
  218.9 234.9 %while.12 = (s32[]{:T(128)}, f32[32,128,128]{2,1,0:T(8,128)}, f32[8,4,256]{2,1,0:T(4,128)S(1)}, s32[8]{0:T(128)S(1)}, s32[32,1,9]{2,0,1:T(8,128)S(1)}, /*index=5...) while((s32[]{:T(128)}, f32[32,128,128]{2,1,0:T(8,128)}, ...), condition=%wide.region_3.4_spmd, body=%wide.region_0.3_spmd.sunk | while | flops 633674496 | bytes 35997664 | solution.py:110
  223.7 1.1 reshape.307
  225.5 2.9 fusion.49
  229.1 4.2 fusion.51
  233.3 3.5 reshape.308
  236.8 1.7 copy.100
  238.6 9.6 %scatter_fusion = f32[32,128,128]{2,1,0:T(8,128)} fusion(f32[32,128,128]{2,1,0:T(8,128)} %get-tuple-element.276, s32[36]{0:T(128)S(1)} %fusion.47, f32[36,128,128]{2,1,0:T(8,128)} %bitcast.107), kind=kCustom, calls=%fused_computation.3.clone.1 | custom fusion | flops 589824 | bytes 7078032 | tf_op jit(solution)/shard_map/while/body/eval_jaxpr/scatter-add | solution.py:106
  253.0 1.1 reshape.307
  254.8 2.9 fusion.49
  258.4 4.2 fusion.51
  262.7 3.5 reshape.308
  266.1 1.7 copy.100
  267.9 9.7 %scatter_fusion = f32[32,128,128]{2,1,0:T(8,128)} fusion(f32[32,128,128]{2,1,0:T(8,128)} %get-tuple-element.276, s32[36]{0:T(128)S(1)} %fusion.47, f32[36,128,128]{2,1,0:T(8,128)} %bitcast.107), kind=kCustom, calls=%fused_computation.3.clone.1 | custom fusion | flops 589824 | bytes 7078032 | tf_op jit(solution)/shard_map/while/body/eval_jaxpr/scatter-add | solution.py:106
  282.4 1.1 reshape.307
  284.2 2.9 fusion.49
  287.9 4.2 fusion.51
  292.1 3.5 reshape.308
  295.5 1.7 copy.100
  297.3 9.7 %scatter_fusion = f32[32,128,128]{2,1,0:T(8,128)} fusion(f32[32,128,128]{2,1,0:T(8,128)} %get-tuple-element.276, s32[36]{0:T(128)S(1)} %fusion.47, f32[36,128,128]{2,1,0:T(8,128)} %bitcast.107), kind=kCustom, calls=%fused_computation.3.clone.1 | custom fusion | flops 589824 | bytes 7078032 | tf_op jit(solution)/shard_map/while/body/eval_jaxpr/scatter-add | solution.py:106
  311.9 1.1 reshape.307
  313.7 2.9 fusion.49
  317.3 4.2 fusion.51
  321.5 3.5 reshape.308
  324.9 1.7 copy.100
  326.8 9.7 %scatter_fusion = f32[32,128,128]{2,1,0:T(8,128)} fusion(f32[32,128,128]{2,1,0:T(8,128)} %get-tuple-element.276, s32[36]{0:T(128)S(1)} %fusion.47, f32[36,128,128]{2,1,0:T(8,128)} %bitcast.107), kind=kCustom, calls=%fused_computation.3.clone.1 | custom fusion | flops 589824 | bytes 7078032 | tf_op jit(solution)/shard_map/while/body/eval_jaxpr/scatter-add | solution.py:106
  341.3 1.1 reshape.307
  343.1 2.9 fusion.49
  346.7 4.2 fusion.51
  350.9 3.5 reshape.308
  354.4 1.7 copy.100
  356.2 9.7 %scatter_fusion = f32[32,128,128]{2,1,0:T(8,128)} fusion(f32[32,128,128]{2,1,0:T(8,128)} %get-tuple-element.276, s32[36]{0:T(128)S(1)} %fusion.47, f32[36,128,128]{2,1,0:T(8,128)} %bitcast.107), kind=kCustom, calls=%fused_computation.3.clone.1 | custom fusion | flops 589824 | bytes 7078032 | tf_op jit(solution)/shard_map/while/body/eval_jaxpr/scatter-add | solution.py:106
  372.4 2.9 fusion.49
  376.0 4.2 fusion.51
  380.2 3.5 reshape.308
  383.7 1.7 copy.100
  385.5 9.6 %scatter_fusion = f32[32,128,128]{2,1,0:T(8,128)} fusion(f32[32,128,128]{2,1,0:T(8,128)} %get-tuple-element.276, s32[36]{0:T(128)S(1)} %fusion.47, f32[36,128,128]{2,1,0:T(8,128)} %bitcast.107), kind=kCustom, calls=%fused_computation.3.clone.1 | custom fusion | flops 589824 | bytes 7078032 | tf_op jit(solution)/shard_map/while/body/eval_jaxpr/scatter-add | solution.py:106
  400.0 1.1 reshape.307
  401.8 2.9 fusion.49
  405.4 4.2 fusion.51
  409.6 3.5 reshape.308
  413.1 1.7 copy.100
  414.9 9.6 %scatter_fusion = f32[32,128,128]{2,1,0:T(8,128)} fusion(f32[32,128,128]{2,1,0:T(8,128)} %get-tuple-element.276, s32[36]{0:T(128)S(1)} %fusion.47, f32[36,128,128]{2,1,0:T(8,128)} %bitcast.107), kind=kCustom, calls=%fused_computation.3.clone.1 | custom fusion | flops 589824 | bytes 7078032 | tf_op jit(solution)/shard_map/while/body/eval_jaxpr/scatter-add | solution.py:106
  429.3 1.1 reshape.307
  431.1 2.9 fusion.49
  434.7 4.2 fusion.51
  438.9 3.5 reshape.308
  442.4 1.7 copy.100
  444.2 9.6 %scatter_fusion = f32[32,128,128]{2,1,0:T(8,128)} fusion(f32[32,128,128]{2,1,0:T(8,128)} %get-tuple-element.276, s32[36]{0:T(128)S(1)} %fusion.47, f32[36,128,128]{2,1,0:T(8,128)} %bitcast.107), kind=kCustom, calls=%fused_computation.3.clone.1 | custom fusion | flops 589824 | bytes 7078032 | tf_op jit(solution)/shard_map/while/body/eval_jaxpr/scatter-add | solution.py:106
  453.8 7.3 all-to-all-start.2
  462.0 1.5 fusion.21
  464.8 43.7 %all-to-all-done.2 = f32[16,2,128,128]{3,2,1,0:T(8,128)S(1)} async-done(((f32[16,2,128,128]{3,2,1,0:T(8,128)}), f32[16,2,128,128]{3,2,1,0:T(8,128)S(1)}, u32[]{:S(2)}, u32[]{:S(2)}) %all-to-all-start.2) | async-done | bytes 2097184 | tf_op jit(solution)/shard_map/all_to_all | solution.py:112
  508.7 2.7 scatter_fusion.1
  512.3 176.1 %reduce-scatter.2.cloned.1.call-done = f32[32,256]{1,0:T(8,128)} async-done(((f32[1024,256]{1,0:T(8,128)}), f32[32,256]{1,0:T(8,128)}) %reduce-scatter.2.cloned.1.call-update) | async-done | bytes 32784 | tf_op jit(solution)/shard_map/reduce_scatter | solution.py:132
  688.4 1.4 copy.66
  689.8 161.4 %all-reduce.2.cloned.1.call-done = f32[16,128,128]{2,1,0:T(8,128)} async-done(((f32[16,128,128]{2,1,0:T(8,128)}), f32[16,128,128]{2,1,0:T(8,128)}) %all-reduce.2.cloned.1.call-update) | async-done | bytes 1048592 | tf_op jit(solution)/shard_map/psum | solution.py:124
  851.2 2.3 copy.114
  (237 shorter events, 51.7 us)
Async XLA Ops:
  13.6 10.5 %copy-start.3 = (f32[32,1,256]{2,1,0:T(1,128)S(1)}, f32[32,1,256]{2,1,0:T(1,128)}, u32[]{:S(2)}) copy-start(f32[32,1,256]{2,1,0:T(1,128)} %param.17) | copy-start | bytes 98308
  13.6 11.2 %copy-start.5 = (s32[1,1,16,2]{2,3,1,0:T(2,128)S(1)}, s32[1,1,16,2]{2,3,1,0:T(2,128)}, u32[]{:S(2)}) copy-start(s32[1,1,16,2]{2,3,1,0:T(2,128)} %param.20) | copy-start | bytes 388
  13.6 11.5 %copy-start.4 = (s32[32,1,9]{0,1,2:T(1,128)S(1)}, s32[32,1,9]{0,1,2:T(1,128)}, u32[]{:S(2)}) copy-start(s32[32,1,9]{0,1,2:T(1,128)} %param.21) | copy-start | bytes 3460
  13.6 193.1 %all-to-all-start.1 = ((bf16[16,16,128,128]{3,2,1,0:T(8,128)(2,1)}), bf16[16,16,128,128]{3,2,1,0:T(8,128)(2,1)}, u32[]{:S(2)}, u32[]{:S(2)}) async-start(bf16[16,16,128,128]{3,2,1,0:T(8,128)(2,1)} %stack.2), calls=%async_computation.1 | async-start | bytes 16777216 | tf_op jit(solution)/shard_map/all_to_all | solution.py:13
  24.0 88.4 %all-gather.3.cloned.1.call-start = ((), (), s32[]{:S(2)}) async-start(), calls=%async_computation.6 | async-start | bytes 1081344 | tf_op jit(solution)/shard_map/all_gather | solution.py:62
  206.7 247.2 %all-to-all-start = ((s32[16,1,2]{2,1,0:T(1,128)}), s32[16,1,2]{2,1,0:T(1,128)S(1)}, u32[]{:S(2)}, u32[]{:S(2)}) async-start(s32[16,1,2]{2,1,0:T(1,128)} %copy.56), calls=%async_computation | async-start | bytes 16384 | tf_op jit(solution)/shard_map/all_to_all | solution.py:65
  218.9 3.8 copy-start
  238.6 9.7 %copy-start.1 = (bf16[32,128,128]{2,1,0:T(8,128)(2,1)S(1)}, bf16[32,128,128]{2,1,0:T(8,128)(2,1)}, u32[]{:S(2)}) copy-start(bf16[32,128,128]{2,1,0:T(8,128)(2,1)} %copy-done) | copy-start | bytes 3145732 | tf_op jit(solution)/shard_map/while
  248.2 3.8 copy-start
  267.9 9.7 %copy-start.1 = (bf16[32,128,128]{2,1,0:T(8,128)(2,1)S(1)}, bf16[32,128,128]{2,1,0:T(8,128)(2,1)}, u32[]{:S(2)}) copy-start(bf16[32,128,128]{2,1,0:T(8,128)(2,1)} %copy-done) | copy-start | bytes 3145732 | tf_op jit(solution)/shard_map/while
  277.6 3.8 copy-start
  297.3 9.7 %copy-start.1 = (bf16[32,128,128]{2,1,0:T(8,128)(2,1)S(1)}, bf16[32,128,128]{2,1,0:T(8,128)(2,1)}, u32[]{:S(2)}) copy-start(bf16[32,128,128]{2,1,0:T(8,128)(2,1)} %copy-done) | copy-start | bytes 3145732 | tf_op jit(solution)/shard_map/while
  307.1 3.8 copy-start
  326.8 9.7 %copy-start.1 = (bf16[32,128,128]{2,1,0:T(8,128)(2,1)S(1)}, bf16[32,128,128]{2,1,0:T(8,128)(2,1)}, u32[]{:S(2)}) copy-start(bf16[32,128,128]{2,1,0:T(8,128)(2,1)} %copy-done) | copy-start | bytes 3145732 | tf_op jit(solution)/shard_map/while
  336.5 3.8 copy-start
  356.2 9.7 %copy-start.1 = (bf16[32,128,128]{2,1,0:T(8,128)(2,1)S(1)}, bf16[32,128,128]{2,1,0:T(8,128)(2,1)}, u32[]{:S(2)}) copy-start(bf16[32,128,128]{2,1,0:T(8,128)(2,1)} %copy-done) | copy-start | bytes 3145732 | tf_op jit(solution)/shard_map/while
  365.8 3.8 copy-start
  385.5 9.6 %copy-start.1 = (bf16[32,128,128]{2,1,0:T(8,128)(2,1)S(1)}, bf16[32,128,128]{2,1,0:T(8,128)(2,1)}, u32[]{:S(2)}) copy-start(bf16[32,128,128]{2,1,0:T(8,128)(2,1)} %copy-done) | copy-start | bytes 3145732 | tf_op jit(solution)/shard_map/while
  395.2 3.8 copy-start
  414.9 9.7 %copy-start.1 = (bf16[32,128,128]{2,1,0:T(8,128)(2,1)S(1)}, bf16[32,128,128]{2,1,0:T(8,128)(2,1)}, u32[]{:S(2)}) copy-start(bf16[32,128,128]{2,1,0:T(8,128)(2,1)} %copy-done) | copy-start | bytes 3145732 | tf_op jit(solution)/shard_map/while
  424.5 3.8 copy-start
  444.2 9.6 %copy-start.1 = (bf16[32,128,128]{2,1,0:T(8,128)(2,1)S(1)}, bf16[32,128,128]{2,1,0:T(8,128)(2,1)}, u32[]{:S(2)}) copy-start(bf16[32,128,128]{2,1,0:T(8,128)(2,1)} %copy-done) | copy-start | bytes 3145732 | tf_op jit(solution)/shard_map/while
  453.8 54.7 %all-to-all-start.2 = ((f32[16,2,128,128]{3,2,1,0:T(8,128)}), f32[16,2,128,128]{3,2,1,0:T(8,128)S(1)}, u32[]{:S(2)}, u32[]{:S(2)}) async-start(f32[16,2,128,128]{3,2,1,0:T(8,128)} %bitcast.109), calls=%async_computation.2 | async-start | bytes 4194304 | tf_op jit(solution)/shard_map/all_to_all | solution.py:112
  461.2 227.3 %reduce-scatter.2.cloned.1.call-start = ((), (), s32[]{:S(2)}) async-start(), calls=%async_computation.5 | async-start | bytes 1081344 | tf_op jit(solution)/shard_map/reduce_scatter | solution.py:132
  463.5 387.7 %all-reduce.2.cloned.1.call-start = ((), (), s32[]{:S(2)}) async-start(), calls=%async_computation.4 | async-start | bytes 2097152 | tf_op jit(solution)/shard_map/psum | solution.py:124
  511.3 1.0 copy-start.2
Sparse Core Ops, SparseCore 0:
  28.6 83.7 all-gather.2
  466.4 221.9 reduce-scatter.1
  692.5 158.7 all-reduce.1
